TPU v7x, 256 devices: a whole 4x4x8 slice. The times are simulated.
256 devices in a mesh: wide: 32 (over x, y, core), narrow: 8 (over z).
Axes of the slice: x: 4, y: 4, z: 8, core: 2. Of those that a mesh axis runs over, the one named last changes fastest.
Arguments:
- events: bfloat16 [32768, 1024], P('wide'), may hold values from -36 to 36
- lengths: int32 [24], replicated, may hold values from 1 to 8192, 32768 in all
- in_gain: float32 [1024], replicated, may hold values from 0.1 to 1.9
- w_uvqk: bfloat16 [1024, 8, 512], P(None, 'narrow'), may hold values from -2 to 2, as said below
- out_gain: float32 [8, 128], P('narrow'), may hold values from 0.1 to 1.9
- w_out: bfloat16 [8, 128, 1024], P('narrow'), may hold values from -0.25 to 0.25
Outputs:
- layer_out: bfloat16 [32768, 1024], P('wide', 'narrow')
Inputs may be any that keep to these rules, and one draw needn't show every extreme that they name: `w_uvqk`: projection weights.
All inputs are finite; a program needn't handle non-finite values.
Results may differ from a plain program's by a relative error of at most 0.0036.
Values may be sent and summed in bfloat16 or wider, within the bound.
No kernel may reach another device: no remote copies, remote signals or barrier semaphores. Data moves between devices by JAX's collectives and lax.ppermute only.
A program may use at most 64 MiB of HBM per device.

v0:
```python
import functools

import jax
import jax.numpy as jnp
from jax import lax
from jax.experimental import pallas as pl
from jax.experimental.pallas import tpu as pltpu
from jax.sharding import PartitionSpec as P

F32 = jnp.float32
BF16 = jnp.bfloat16
SMEM = pl.BlockSpec(memory_space=pltpu.SMEM)
VMEM = pl.BlockSpec(memory_space=pltpu.VMEM)
ROWS = 1024
DH = 128
HALF = 512
TQ = 512
TK = 256
NT = (((1,), (1,)), ((), ()))


def silu(x):
    half = 0.5 * x
    return half + half * jnp.tanh(half)


def kept(*values):
    return [pltpu.with_memory_space_constraint(value, pltpu.VMEM) for value in values]


def project_kernel(
    parts, events_hbm, gain_hbm, w_hbm, kv_hbm, q_ref, u_hbm, events, gain, w, kv_ref, u_ref, sems, out_sems
):
    rows = events.shape[0] // parts
    fetch_w = pltpu.make_async_copy(w_hbm, w, sems.at[parts])
    fetch_gain = pltpu.make_async_copy(gain_hbm, gain, sems.at[parts + 1])
    fetches = [
        pltpu.make_async_copy(
            events_hbm.at[pl.ds(part * rows, rows)], events.at[pl.ds(part * rows, rows)], sems.at[part]
        )
        for part in range(parts)
    ]
    fetches[0].start()
    fetch_gain.start()
    fetch_w.start()
    for fetch in fetches[1:]:
        fetch.start()
    stores = []
    for part in range(parts):
        fetches[part].wait()
        x = events[part * rows : (part + 1) * rows, :].astype(F32)
        average = jnp.mean(x, axis=-1, keepdims=True)
        centred = x - average
        variance = jnp.mean(centred * centred, axis=-1, keepdims=True)
        if part == 0:
            fetch_gain.wait()
        normed = (centred * lax.rsqrt(variance + 1e-05) * gain[...]).astype(BF16)
        if part == 0:
            fetch_w.wait()
        out = silu(jnp.dot(normed, w[...], preferred_element_type=F32)).astype(BF16)
        at = slice(part * rows, (part + 1) * rows)
        u_ref[at, :] = out[:, :DH]
        q_ref[at, :] = out[:, 2 * DH : 3 * DH]
        keys, values = out[:, 3 * DH :], out[:, DH : 2 * DH]
        kv_ref[at, :DH] = keys
        kv_ref[at, DH:] = values
        at = pl.ds(part * rows, rows)
        for index, (value_ref, value_hbm) in enumerate(((kv_ref, kv_hbm), (u_ref, u_hbm))):
            store = pltpu.make_async_copy(value_ref.at[at], value_hbm.at[at], out_sems.at[part, index])
            store.start()
            stores.append(store)
    for store in stores:
        store.wait()


def project(events, in_gain, w):
    rows, width = events.shape
    parts = 4
    hbm = pl.BlockSpec(memory_space=pltpu.HBM)
    return pl.pallas_call(
        functools.partial(project_kernel, parts),
        in_specs=[hbm] * 3,
        out_specs=[hbm, VMEM, hbm],
        out_shape=[
            pltpu.HBM((rows, 2 * DH), BF16),
            pltpu.VMEM((rows, DH), BF16),
            pltpu.HBM((rows, DH), BF16),
        ],
        scratch_shapes=[
            pltpu.VMEM((rows, width), BF16),
            pltpu.VMEM((1, width), F32),
            pltpu.VMEM((width, 4 * DH), BF16),
            pltpu.VMEM((rows, 2 * DH), BF16),
            pltpu.VMEM((rows, DH), BF16),
            pltpu.SemaphoreType.DMA((parts + 2,)),
            pltpu.SemaphoreType.DMA((parts, 2)),
        ],
        cost_estimate=pl.CostEstimate(
            flops=2 * rows * width * 4 * DH, bytes_accessed=4 << 20, transcendentals=rows * 4 * DH
        ),
        compiler_params=pltpu.CompilerParams(vmem_limit_bytes=20 << 20),
        name="project",
    )(*[pltpu.with_memory_space_constraint(value, pltpu.HBM) for value in (events, in_gain[None], w)])


def attend_kernel(users, pieces, count, first, last, place_ref, lengths_ref, q_own, q_sib, *refs):
    blocks, refs = refs[:count], refs[count:]
    if first:
        out_hbm, total_out, starts_ref, spread_ref, q_ref, total_ref, sems = refs
        outs = [total_out]
        copies, _, half = spread_ref.shape
        columns = pl.ds(pl.multiple_of(place_ref[0] % 2 * half, half), half)
        spreads = [
            pltpu.make_async_copy(out_hbm.at[0, :, columns], spread_ref.at[copy], sems.at[copy])
            for copy in range(copies)
        ]
        for spread in spreads:
            spread.start()
    else:
        starts_ref, carried = refs[:2]
        outs, (q_ref, total_ref) = refs[2:-2], refs[-2:]
    me = place_ref[0]
    scale = 0.5 * DH ** (-0.5)

    def weigh(scores):
        half = scores * scale
        return half + half * jnp.tanh(half)

    q_ref[:ROWS, :] = q_own[...]
    q_ref[ROWS:, :] = q_sib[...]
    if first:
        total_ref[...] = jnp.zeros_like(total_ref)
    else:
        total_ref[...] = carried[...]

    def one_part(part, nothing):
        side, inner = part // (ROWS // TQ), part % (ROWS // TQ)
        q_first = jnp.where(side == 0, me, me + 1 - 2 * (me % 2)) * ROWS + inner * TQ
        q_last = q_first + TQ - 1
        rows = pl.ds(pl.multiple_of(part * TQ, TQ), TQ)
        end = jnp.int32(0)
        low = jnp.int32(0)
        high = jnp.int32(0)
        for user in range(users):
            end = end + lengths_ref[user]
            low = jnp.where(end <= q_first, end, low)
            high = jnp.where(end <= q_last, end, high)
        if first:
            starts_ref[rows, :] = jnp.full((TQ, DH), low, jnp.int32)
            end = jnp.int32(0)
            for user in range(users):
                end = end + lengths_ref[user]

                @pl.when((end > q_first) & (end <= q_last))
                def _(end=end):
                    after = q_first + lax.broadcasted_iota(jnp.int32, (TQ, DH), 0) >= end
                    starts_ref[rows, :] = jnp.where(after, end, starts_ref[rows, :])

        for block, offset, back in pieces:
            kv_ref = blocks[block]
            k_first = (me - back) * ROWS + offset
            reached = (me >= back) & (k_first + HALF > low) & (k_first <= q_last)
            whole = (k_first >= high) & (k_first + HALF - 1 <= q_first)

            @pl.when(reached & whole)
            def _():
                q = q_ref[rows, :]
                weights = []
                for piece in range(HALF // TK):
                    keys = kv_ref[offset + piece * TK : offset + (piece + 1) * TK, :DH]
                    scores = lax.dot_general(q, keys, NT, preferred_element_type=F32)
                    weights.append(weigh(scores).astype(BF16))
                values = kv_ref[offset : offset + HALF, DH:]
                total_ref[rows, :] += jnp.dot(
                    jnp.concatenate(weights, axis=1), values, preferred_element_type=F32
                )

            @pl.when(reached & jnp.logical_not(whole))
            def _():
                q = q_ref[rows, :]
                begin = jnp.maximum(low - k_first, 0) // TK
                stop = jnp.minimum((q_last - k_first) // TK + 1, HALF // TK)
                q_start = starts_ref[rows, :]
                q_pos = q_first + lax.broadcasted_iota(jnp.int32, (TQ, DH), 0)

                def step(piece, carry):
                    at = pl.multiple_of(offset + piece * TK, TK)
                    keys = kv_ref[pl.ds(at, TK), :DH]
                    values = kv_ref[pl.ds(at, TK), DH:]
                    scores = lax.dot_general(q, keys, NT, preferred_element_type=F32)
                    lanes = lax.broadcasted_iota(jnp.int32, (TQ, DH), 1) + (k_first + piece * TK)
                    allowed = []
                    for strip in range(TK // DH):
                        k_pos = lanes + strip * DH
                        keep = (k_pos >= q_start) & (k_pos <= q_pos)
                        allowed.append(
                            jnp.where(keep, weigh(scores[:, strip * DH : (strip + 1) * DH]), 0.0)
                        )
                    weights = jnp.concatenate(allowed, axis=1).astype(BF16)
                    total_ref[rows, :] += jnp.dot(weights, values, preferred_element_type=F32)
                    return carry

                lax.fori_loop(begin, stop, step, 0)

        return nothing

    lax.fori_loop(0, 2 * ROWS // TQ, one_part, 0)
    if first:
        for spread in spreads:
            spread.wait()
    if last:
        outs[0][...] = total_ref[:ROWS, :]
        outs[1][...] = total_ref[ROWS:, :].astype(BF16)
    else:
        outs[0][...] = total_ref[...]


def attend(place, lengths, q_own, q_sib, blocks, carried=None, weight=1, last=False, w_out=None, copies=1):
    count = len(blocks)
    first = carried is None
    pieces = [
        (index, offset, back)
        for index, (block, back) in enumerate(blocks)
        for offset in range(0, block.shape[0], HALF)
    ]
    if first:
        outs = [
            pltpu.VMEM((2 * ROWS, DH), F32),
            pltpu.VMEM((2 * ROWS, DH), jnp.int32),
            pltpu.HBM((copies, DH, w_out.shape[2] // 2), BF16),
        ]
    elif last:
        outs = [pltpu.VMEM((ROWS, DH), F32), pltpu.VMEM((ROWS, DH), BF16)]
    else:
        outs = [pltpu.VMEM((2 * ROWS, DH), F32)]
    arrays = kept(q_own, q_sib, *[block[0] for block in blocks], *(() if first else carried))
    specs = [SMEM, SMEM] + [VMEM] * len(arrays)
    scratch = [pltpu.VMEM((2 * ROWS, DH), BF16), pltpu.VMEM((2 * ROWS, DH), F32)]
    if first:
        arrays.append(pltpu.with_memory_space_constraint(w_out, pltpu.HBM))
        specs.append(pl.BlockSpec(memory_space=pltpu.HBM))
        scratch.append(pltpu.SemaphoreType.DMA((copies,)))
    return pl.pallas_call(
        functools.partial(attend_kernel, lengths.shape[0], pieces, count, first, last),
        in_specs=specs,
        out_specs=[VMEM, VMEM, pl.BlockSpec(memory_space=pltpu.HBM)] if first else [VMEM] * len(outs),
        out_shape=outs,
        scratch_shapes=scratch,
        compiler_params=pltpu.CompilerParams(vmem_limit_bytes=20 << 20),
        cost_estimate=pl.CostEstimate(
            flops=weight * len(pieces) * 4 * ROWS * ROWS * DH,
            bytes_accessed=4 << 20,
            transcendentals=weight * len(pieces) * ROWS * ROWS,
        ),
        name="attend",
    )(place, lengths, *arrays)


def gate_kernel(own_ref, sib_ref, u_ref, gain_ref, out_ref):
    attended = own_ref[...] + sib_ref[...].astype(F32)
    centre = jnp.mean(attended, axis=-1, keepdims=True)
    centred = attended - centre
    deviation = jnp.mean(centred * centred, axis=-1, keepdims=True)
    gated = centred * lax.rsqrt(deviation + 1e-05) * gain_ref[...] * u_ref[...].astype(F32)
    out_ref[...] = gated.astype(BF16)


def gate(own, sib, u, gain):
    return pl.pallas_call(
        gate_kernel,
        in_specs=[VMEM] * 4,
        out_specs=VMEM,
        out_shape=pltpu.VMEM(u.shape, BF16),
        compiler_params=pltpu.CompilerParams(vmem_limit_bytes=8 << 20),
        name="gate",
    )(*kept(own, sib), u, gain)


def combine_kernel(heads, place_ref, gated_ref, mine_ref, other_ref, events_hbm, out_ref, events, sem):
    share = events.shape[0]
    fetch = pltpu.make_async_copy(
        events_hbm.at[pl.ds(pl.multiple_of(place_ref[1] * share, share), share)], events, sem
    )
    fetch.start()
    gated = jnp.concatenate([gated_ref[head] for head in range(heads)], axis=1)
    half = heads // 2
    core = place_ref[0] % 2
    totals = [
        jnp.dot(gated, w_ref[...].reshape(heads * DH, half * DH), preferred_element_type=F32)
        for w_ref in (mine_ref, other_ref)
    ]
    fetch.wait()
    for total, side in zip(totals, (core, 1 - core)):
        columns = pl.ds(pl.multiple_of(side * half * DH, half * DH), half * DH)
        total = (total + events[:, columns].astype(F32)).astype(BF16)
        for part in range(half):
            out_ref[side * half + part] = total[:, part * DH : (part + 1) * DH]


def combine(place, gated, mine, other, events):
    heads, share = gated.shape[:2]
    return pl.pallas_call(
        functools.partial(combine_kernel, heads),
        in_specs=[SMEM] + [VMEM] * 3 + [pl.BlockSpec(memory_space=pltpu.HBM)],
        out_specs=VMEM,
        out_shape=pltpu.VMEM(gated.shape, BF16),
        scratch_shapes=[pltpu.VMEM((share, events.shape[1]), BF16), pltpu.SemaphoreType.DMA],
        compiler_params=pltpu.CompilerParams(vmem_limit_bytes=8 << 20),
        name="combine",
    )(place, *kept(gated, mine, other), pltpu.with_memory_space_constraint(events, pltpu.HBM))


def on_device(events, lengths, in_gain, w_uvqk, out_gain, w_out):
    rows = events.shape[0]
    heads = lax.axis_size("narrow")
    count = lax.axis_size("wide")
    place = jnp.stack([lax.axis_index("wide"), lax.axis_index("narrow")]).astype(jnp.int32)

    def moved(value, steps):
        pairs = [(i, (i + steps) % count) for i in range(count)]
        return lax.ppermute(value, "wide", pairs)

    def swapped(value):
        return lax.ppermute(value, "wide", [(i, i ^ 1) for i in range(count)])

    kv, q, u = project(events, in_gain, w_uvqk[:, 0, :])
    q_sib = swapped(q)
    back1 = moved(kv, 2)
    back4 = moved(kv, 8)
    acc, starts, spread = attend(
        place, lengths, q, q_sib, [(kv, 0)], weight=0, w_out=w_out, copies=heads
    )
    spread, acc = lax.optimization_barrier((spread, acc))
    w_half = lax.all_to_all(spread, "narrow", 0, 0)
    back1, acc = lax.optimization_barrier((back1, acc))
    back2 = moved(back1, 2)
    back3 = moved(back4, -2)
    acc = attend(place, lengths, q, q_sib, [(back1, 2), (back4, 8)], (starts, acc), weight=0)[0]
    acc = attend(place, lengths, q, q_sib, [(back2, 4)], (starts, acc), weight=50)[0]
    own, sib = attend(place, lengths, q, q_sib, [(back3, 6)], (starts, acc), weight=50, last=True)
    gated = gate(own, swapped(sib), u, out_gain)
    w_half, gated = lax.optimization_barrier((w_half, gated))
    w_other = swapped(w_half)
    gated = lax.all_to_all(gated.reshape(heads, rows // heads, DH), "narrow", 0, 0)
    out = combine(place, gated, w_half, w_other, events)
    return lax.all_to_all(out, "narrow", 0, 0).reshape(rows, DH)


def solution(mesh):
    in_specs = (
        P("wide", None),
        P(),
        P(),
        P(None, "narrow", None),
        P("narrow", None),
        P("narrow", None, None),
    )
    out_specs = P("wide", "narrow")
    return jax.shard_map(
        on_device, mesh=mesh, in_specs=in_specs, out_specs=out_specs, check_vma=False
    )
```

profile of v0, /device:TPU:1, one launch (start us, length us, event | category | flops | bytes accessed | tf_op | source)
XLA Modules:
  0.0 115.4 jit_solution(8029431687006769424)
XLA Ops:
  0.0 4.9 %project.1 = (bf16[1024,256]{1,0:T(8,128)(2,1)}, bf16[1024,128]{1,0:T(8,128)(2,1)S(1)}, bf16[1024,128]{1,0:T(8,128)(2,1)}) custom-call(bf16[1024,1024]{1,0:T(8,128)(2,1)} %events_hbm.3, f32[1,1024]{1,0:T(1,128)} %bitcast.9, bf16[1024,512]{1,0:T(8,128)(2,1)} %bitcast.8), custom_call_target="tpu_custom_call" | custom-call | flops 1073741824 | bytes 4194304 | tf_op jit(solution)/shard_map/project/pallas_call | solution.py:80
  4.9 2.2 %collective-permute-start.3 = (bf16[1024,256]{1,0:T(8,128)(2,1)}, bf16[1024,256]{1,0:T(8,128)(2,1)}, u32[]{:S(2)}, u32[]{:S(2)}) collective-permute-start(bf16[1024,256]{1,0:T(8,128)(2,1)} %get-tuple-element.20.refs_0_), channel_id=1, source_target_pairs={{0,16},{8,24},{16,32},{24,40},{32,48},{40,56},{48,64},{56,72},{64,... | collective-permute-start | bytes 1572872 | tf_op jit(solution)/shard_map/ppermute | solution.py:321
  7.1 1.2 %collective-permute-start = (bf16[1024,128]{1,0:T(8,128)(2,1)S(1)}, bf16[1024,128]{1,0:T(8,128)(2,1)S(1)}, u32[]{:S(2)}, u32[]{:S(2)}) collective-permute-start(bf16[1024,128]{1,0:T(8,128)(2,1)S(1)} %get-tuple-element.19.q_own), channel_id=1, source_target_pairs={{0,8},{8,0},{16,24},{24,16},{32,40},{40,32},{48,56},{56,48},{64,72... | collective-permute-start | bytes 786440 | tf_op jit(solution)/shard_map/ppermute | solution.py:324
  8.3 1.0 collective-permute-start.1
  9.5 1.0 copy-done.2
  10.5 33.6 %attend.4 = (f32[2048,128]{1,0:T(8,128)S(1)}, s32[2048,128]{1,0:T(8,128)S(1)}, bf16[8,128,512]{2,1,0:T(8,128)(2,1)}) custom-call(s32[2]{0:T(128)S(1)} %pad_add_fusion.place_ref, s32[24]{0:T(128)S(1)} %copy-done.4, bf16[1024,128]{1,0:T(8,128)(2,1)S(1)} %get-tuple-element.19.q_own, bf16[1024,128]{1,0:T(8,128)(2,1)S(1)} %collective-permute-done.q_sib, ...), custom_call_target="tpu_custom_call" | custom-call | bytes 4194304 | tf_op jit(solution)/shard_map/attend/pallas_call | solution.py:243
  44.1 1.2 %collective-permute-start.4 = (bf16[1024,256]{1,0:T(8,128)(2,1)}, bf16[1024,256]{1,0:T(8,128)(2,1)}, u32[]{:S(2)}, u32[]{:S(2)}) collective-permute-start(bf16[1024,256]{1,0:T(8,128)(2,1)} %collective-permute-done.3.refs_0_), channel_id=1, source_target_pairs={{0,16},{8,24},{16,32},{24,40},{32,48},{40,56},{48,64},{56,72},{64,... | collective-permute-start | bytes 1572872 | tf_op jit(solution)/shard_map/ppermute | solution.py:321
  45.4 8.2 %all-to-all-start = ((bf16[8,128,512]{2,1,0:T(8,128)(2,1)}), bf16[8,128,512]{2,1,0:T(8,128)(2,1)S(1)}, u32[]{:S(2)}, u32[]{:S(2)}) async-start(bf16[8,128,512]{2,1,0:T(8,128)(2,1)} %get-tuple-element.23), calls=%async_computation | async-start | bytes 2097152 | tf_op jit(solution)/shard_map/all_to_all | solution.py:334
  53.5 3.8 %collective-permute-start.2 = (bf16[1024,256]{1,0:T(8,128)(2,1)}, bf16[1024,256]{1,0:T(8,128)(2,1)S(1)}, u32[]{:S(2)}, u32[]{:S(2)}) collective-permute-start(bf16[1024,256]{1,0:T(8,128)(2,1)} %collective-permute-done.1.refs_1_), channel_id=1, source_target_pairs={{0,240},{8,248},{16,0},{24,8},{32,16},{40,24},{48,32},{56,40},{64,... | collective-permute-start | bytes 1572872 | tf_op jit(solution)/shard_map/ppermute | solution.py:321
  57.3 0.9 copy-done.1
  58.2 1.8 %attend.5.refs_2_ = f32[2048,128]{1,0:T(8,128)S(1)} custom-call(s32[2]{0:T(128)S(1)} %pad_add_fusion.place_ref, s32[24]{0:T(128)S(1)} %copy-done.4, bf16[1024,128]{1,0:T(8,128)(2,1)S(1)} %get-tuple-element.19.q_own, bf16[1024,128]{1,0:T(8,128)(2,1)S(1)} %copy-done.1, bf16[1024,256]{1,0:T(8,128)(2,1)} %collective-permute-done.3.refs_0_, ...), custom_call_target="tpu_custom_call" | custom-call | bytes 4194304 | tf_op jit(solution)/shard_map/attend/pallas_call | solution.py:243
  60.1 1.3 %collective-permute-done.4.refs_0_ = bf16[1024,256]{1,0:T(8,128)(2,1)} collective-permute-done((bf16[1024,256]{1,0:T(8,128)(2,1)}, bf16[1024,256]{1,0:T(8,128)(2,1)}, u32[]{:S(2)}, u32[]{:S(2)}) %collective-permute-start.4) | collective-permute-done | bytes 524320 | tf_op jit(solution)/shard_map/ppermute | solution.py:321
  61.3 1.6 %attend.6.refs_2_ = f32[2048,128]{1,0:T(8,128)S(1)} custom-call(s32[2]{0:T(128)S(1)} %pad_add_fusion.place_ref, s32[24]{0:T(128)S(1)} %copy-done.4, bf16[1024,128]{1,0:T(8,128)(2,1)S(1)} %get-tuple-element.19.q_own, bf16[1024,128]{1,0:T(8,128)(2,1)S(1)} %copy-done.1, bf16[1024,256]{1,0:T(8,128)(2,1)} %collective-permute-done.4.refs_0_, ...), custom_call_target="tpu_custom_call" | custom-call | flops 53687091200 | bytes 4194304 | tf_op jit(solution)/shard_map/attend/pallas_call | solution.py:243
  62.9 5.1 %collective-permute-done.2.refs_0_ = bf16[1024,256]{1,0:T(8,128)(2,1)S(1)} collective-permute-done((bf16[1024,256]{1,0:T(8,128)(2,1)}, bf16[1024,256]{1,0:T(8,128)(2,1)S(1)}, u32[]{:S(2)}, u32[]{:S(2)}) %collective-permute-start.2) | collective-permute-done | bytes 524320 | tf_op jit(solution)/shard_map/ppermute | solution.py:321
  68.0 1.0 attend.7
  69.1 1.8 %collective-permute-start.5 = (bf16[1024,128]{1,0:T(8,128)(2,1)S(1)}, bf16[1024,128]{1,0:T(8,128)(2,1)S(1)}, u32[]{:S(2)}, u32[]{:S(2)}) collective-permute-start(bf16[1024,128]{1,0:T(8,128)(2,1)S(1)} %get-tuple-element.29), channel_id=1, source_target_pairs={{0,8},{8,0},{16,24},{24,16},{32,40},{40,32},{48,56},{56,48},{64,72... | collective-permute-start | bytes 786440 | tf_op jit(solution)/shard_map/ppermute | solution.py:324
  70.9 1.2 %collective-permute-done.5.sib_ref = bf16[1024,128]{1,0:T(8,128)(2,1)S(1)} collective-permute-done((bf16[1024,128]{1,0:T(8,128)(2,1)S(1)}, bf16[1024,128]{1,0:T(8,128)(2,1)S(1)}, u32[]{:S(2)}, u32[]{:S(2)}) %collective-permute-start.5) | collective-permute-done | bytes 262176 | tf_op jit(solution)/shard_map/ppermute | solution.py:324
  72.1 0.4 gate.1
  72.4 10.3 %all-to-all-done.mine_ref = bf16[8,128,512]{2,1,0:T(8,128)(2,1)S(1)} async-done(((bf16[8,128,512]{2,1,0:T(8,128)(2,1)}), bf16[8,128,512]{2,1,0:T(8,128)(2,1)S(1)}, u32[]{:S(2)}, u32[]{:S(2)}) %all-to-all-start) | async-done | bytes 1048608 | tf_op jit(solution)/shard_map/all_to_all | solution.py:334
  82.8 0.5 collective-permute-start.6
  83.3 14.8 %all_to_all.15.gated_ref = bf16[8,128,128]{2,1,0:T(8,128)(2,1)S(1)} all-to-all(bf16[8,128,128]{2,1,0:T(8,128)(2,1)S(1)} %bitcast.6), channel_id=1, replica_groups=mesh['wide'=32,'narrow'=8] {'narrow'}, dimensions={0} | all-to-all | bytes 524288 | tf_op jit(solution)/shard_map/all_to_all | solution.py:344
  98.1 2.0 %combine.1 = bf16[8,128,128]{2,1,0:T(8,128)(2,1)S(1)} custom-call(s32[2]{0:T(128)S(1)} %pad_add_fusion.place_ref, bf16[8,128,128]{2,1,0:T(8,128)(2,1)S(1)} %all_to_all.15.gated_ref, bf16[8,128,512]{2,1,0:T(8,128)(2,1)S(1)} %all-to-all-done.mine_ref, bf16[8,128,512]{2,1,0:T(8,128)(2,1)S(1)} %collective-permute-done.6.other_ref, bf16[1024,1024]{1,0:T(8,128)(2,1)} %events_hbm.3), custom_call_target="tpu_custom_call" | custom-call | tf_op jit(solution)/shard_map/combine/pallas_call | solution.py:302
  100.0 14.7 %all_to_all.16 = bf16[8,128,128]{2,1,0:T(8,128)(2,1)S(1)} all-to-all(bf16[8,128,128]{2,1,0:T(8,128)(2,1)S(1)} %combine.1), channel_id=1, replica_groups=mesh['wide'=32,'narrow'=8] {'narrow'}, dimensions={0} | all-to-all | bytes 524288 | tf_op jit(solution)/shard_map/all_to_all | solution.py:346
  114.7 0.7 copy.8
  (15 shorter events, 0.2 us)
Async XLA Ops:
  0.0 9.5 %copy-start.4 = (s32[24]{0:T(128)S(1)}, s32[24]{0:T(128)}, u32[]{:S(2)}) copy-start(s32[24]{0:T(128)} %lengths_ref.7) | copy-start | bytes 292
  4.9 39.2 %collective-permute-start.3 = (bf16[1024,256]{1,0:T(8,128)(2,1)}, bf16[1024,256]{1,0:T(8,128)(2,1)}, u32[]{:S(2)}, u32[]{:S(2)}) collective-permute-start(bf16[1024,256]{1,0:T(8,128)(2,1)} %get-tuple-element.20.refs_0_), channel_id=1, source_target_pairs={{0,16},{8,24},{16,32},{24,40},{32,48},{40,56},{48,64},{56,72},{64,... | collective-permute-start | bytes 1572872 | tf_op jit(solution)/shard_map/ppermute | solution.py:321
  7.1 2.4 %collective-permute-start = (bf16[1024,128]{1,0:T(8,128)(2,1)S(1)}, bf16[1024,128]{1,0:T(8,128)(2,1)S(1)}, u32[]{:S(2)}, u32[]{:S(2)}) collective-permute-start(bf16[1024,128]{1,0:T(8,128)(2,1)S(1)} %get-tuple-element.19.q_own), channel_id=1, source_target_pairs={{0,8},{8,0},{16,24},{24,16},{32,40},{40,32},{48,56},{56,48},{64,72... | collective-permute-start | bytes 786440 | tf_op jit(solution)/shard_map/ppermute | solution.py:324
  8.3 45.2 %collective-permute-start.1 = (bf16[1024,256]{1,0:T(8,128)(2,1)}, bf16[1024,256]{1,0:T(8,128)(2,1)}, u32[]{:S(2)}, u32[]{:S(2)}) collective-permute-start(bf16[1024,256]{1,0:T(8,128)(2,1)} %get-tuple-element.20.refs_0_), channel_id=1, source_target_pairs={{0,64},{8,72},{16,80},{24,88},{32,96},{40,104},{48,112},{56,120},{... | collective-permute-start | bytes 1572872 | tf_op jit(solution)/shard_map/ppermute | solution.py:321
  9.5 1.0 copy-start.2
  10.5 34.8 %copy-start = (bf16[1024,128]{1,0:T(8,128)(2,1)}, bf16[1024,128]{1,0:T(8,128)(2,1)S(1)}, u32[]{:S(2)}) copy-start(bf16[1024,128]{1,0:T(8,128)(2,1)S(1)} %collective-permute-done.q_sib) | copy-start | bytes 786436
  44.1 17.2 %collective-permute-start.4 = (bf16[1024,256]{1,0:T(8,128)(2,1)}, bf16[1024,256]{1,0:T(8,128)(2,1)}, u32[]{:S(2)}, u32[]{:S(2)}) collective-permute-start(bf16[1024,256]{1,0:T(8,128)(2,1)} %collective-permute-done.3.refs_0_), channel_id=1, source_target_pairs={{0,16},{8,24},{16,32},{24,40},{32,48},{40,56},{48,64},{56,72},{64,... | collective-permute-start | bytes 1572872 | tf_op jit(solution)/shard_map/ppermute | solution.py:321
  45.4 37.4 %all-to-all-start = ((bf16[8,128,512]{2,1,0:T(8,128)(2,1)}), bf16[8,128,512]{2,1,0:T(8,128)(2,1)S(1)}, u32[]{:S(2)}, u32[]{:S(2)}) async-start(bf16[8,128,512]{2,1,0:T(8,128)(2,1)} %get-tuple-element.23), calls=%async_computation | async-start | bytes 2097152 | tf_op jit(solution)/shard_map/all_to_all | solution.py:334
  53.5 14.5 %collective-permute-start.2 = (bf16[1024,256]{1,0:T(8,128)(2,1)}, bf16[1024,256]{1,0:T(8,128)(2,1)S(1)}, u32[]{:S(2)}, u32[]{:S(2)}) collective-permute-start(bf16[1024,256]{1,0:T(8,128)(2,1)} %collective-permute-done.1.refs_1_), channel_id=1, source_target_pairs={{0,240},{8,248},{16,0},{24,8},{32,16},{40,24},{48,32},{56,40},{64,... | collective-permute-start | bytes 1572872 | tf_op jit(solution)/shard_map/ppermute | solution.py:321
  57.3 0.9 copy-start.1
  62.9 9.1 %copy-start.3 = (bf16[1024,128]{1,0:T(8,128)(2,1)S(1)}, bf16[1024,128]{1,0:T(8,128)(2,1)}, u32[]{:S(2)}) copy-start(bf16[1024,128]{1,0:T(8,128)(2,1)} %get-tuple-element.30.u_ref) | copy-start | bytes 786436
  62.9 9.1 %copy-start.5 = (f32[1,128]{1,0:T(1,128)S(1)}, f32[1,128]{1,0:T(1,128)}, u32[]{:S(2)}) copy-start(f32[1,128]{1,0:T(1,128)} %gain_ref.1) | copy-start | bytes 1540
  69.1 3.0 %collective-permute-start.5 = (bf16[1024,128]{1,0:T(8,128)(2,1)S(1)}, bf16[1024,128]{1,0:T(8,128)(2,1)S(1)}, u32[]{:S(2)}, u32[]{:S(2)}) collective-permute-start(bf16[1024,128]{1,0:T(8,128)(2,1)S(1)} %get-tuple-element.29), channel_id=1, source_target_pairs={{0,8},{8,0},{16,24},{24,16},{32,40},{40,32},{48,56},{56,48},{64,72... | collective-permute-start | bytes 786440 | tf_op jit(solution)/shard_map/ppermute | solution.py:324
  82.8 15.3 %collective-permute-start.6 = (bf16[8,128,512]{2,1,0:T(8,128)(2,1)S(1)}, bf16[8,128,512]{2,1,0:T(8,128)(2,1)S(1)}, u32[]{:S(2)}, u32[]{:S(2)}) collective-permute-start(bf16[8,128,512]{2,1,0:T(8,128)(2,1)S(1)} %all-to-all-done.mine_ref), channel_id=1, source_target_pairs={{0,8},{8,0},{16,24},{24,16},{32,40},{40,32},{48,56},{56,48},{64,72... | collective-permute-start | bytes 3145736 | tf_op jit(solution)/shard_map/ppermute | solution.py:324
where the time goes:
time: 116 us; the launch traced here: 115 us
  Pallas kernels  45.2 us (39%)
  blocking collectives  29.5 us (25%)
  starting transfers between devices  19.9 us (17%)
  waiting for transfers between devices  18 us (16%)
  local copies, waits for them, and re-layouts  2.71 us (2%)
    pallas_call x4, Pallas kernels, attend(): pl.pallas_call(functools.partial(attend_kernel, lengths.shape[0], pieces,...  38 us
    all_to_all x1, blocking collectives, on_device(): lax.all_to_all(gated.reshape(heads, rows // heads, DH), 'narrow', 0, 0)  14.8 us
    all_to_all x1, blocking collectives, on_device(): return lax.all_to_all(out, 'narrow', 0, 0).reshape(rows, DH)  14.7 us
    all_to_all x1, waiting for transfers between devices, on_device(): w_half = lax.all_to_all(spread, 'narrow', 0, 0)  10.3 us
    all_to_all x1, starting transfers between devices, on_device(): w_half = lax.all_to_all(spread, 'narrow', 0, 0)  8.18 us
    ppermute x4, starting transfers between devices, moved(): return lax.ppermute(value, 'wide', pairs)  8.15 us
    ppermute x4, waiting for transfers between devices, moved(): return lax.ppermute(value, 'wide', pairs)  6.33 us
    pallas_call x1, Pallas kernels, project(): pl.pallas_call(functools.partial(project_kernel, parts), in_specs=[hbm] *...  4.89 us
  transfers between devices with their start and end apart: 8, of which 5 were waited for; matrix products, arithmetic and copies ran while one was open for 0% of the time, Pallas kernels for 33%

commit v1 on v0

--- a/solution.py
+++ b/solution.py
@@ -29,7 +29,8 @@
 
 
 def project_kernel(
-    parts, events_hbm, gain_hbm, w_hbm, kv_hbm, q_ref, u_hbm, events, gain, w, kv_ref, u_ref, sems, out_sems
+    parts, place_ref, events_hbm, gain_hbm, w_hbm, w_out_hbm, kv_hbm, q_ref, u_hbm, spread_hbm,
+    events, gain, w, w_half, kv_ref, u_ref, sems, out_sems, spread_sems,
 ):
     rows = events.shape[0] // parts
     fetch_w = pltpu.make_async_copy(w_hbm, w, sems.at[parts])
@@ -40,11 +41,15 @@
         )
         for part in range(parts)
     ]
+    half = w_half.shape[1]
+    columns = pl.ds(pl.multiple_of(place_ref[0] % 2 * half, half), half)
+    fetch_half = pltpu.make_async_copy(w_out_hbm.at[0, :, columns], w_half, sems.at[parts + 2])
     fetches[0].start()
     fetch_gain.start()
     fetch_w.start()
     for fetch in fetches[1:]:
         fetch.start()
+    fetch_half.start()
     stores = []
     for part in range(parts):
         fetches[part].wait()
@@ -69,53 +74,57 @@
             store = pltpu.make_async_copy(value_ref.at[at], value_hbm.at[at], out_sems.at[part, index])
             store.start()
             stores.append(store)
+        if part == 0:
+            fetch_half.wait()
+            for copy in range(spread_hbm.shape[0]):
+                store = pltpu.make_async_copy(w_half, spread_hbm.at[copy], spread_sems.at[copy])
+                store.start()
+                stores.append(store)
     for store in stores:
         store.wait()
 
 
-def project(events, in_gain, w):
+def project(place, events, in_gain, w, w_out, copies):
     rows, width = events.shape
     parts = 4
     hbm = pl.BlockSpec(memory_space=pltpu.HBM)
     return pl.pallas_call(
         functools.partial(project_kernel, parts),
-        in_specs=[hbm] * 3,
-        out_specs=[hbm, VMEM, hbm],
+        in_specs=[SMEM] + [hbm] * 4,
+        out_specs=[hbm, VMEM, hbm, hbm],
         out_shape=[
             pltpu.HBM((rows, 2 * DH), BF16),
             pltpu.VMEM((rows, DH), BF16),
             pltpu.HBM((rows, DH), BF16),
+            pltpu.HBM((copies, DH, width // 2), BF16),
         ],
         scratch_shapes=[
             pltpu.VMEM((rows, width), BF16),
             pltpu.VMEM((1, width), F32),
             pltpu.VMEM((width, 4 * DH), BF16),
+            pltpu.VMEM((DH, width // 2), BF16),
             pltpu.VMEM((rows, 2 * DH), BF16),
             pltpu.VMEM((rows, DH), BF16),
-            pltpu.SemaphoreType.DMA((parts + 2,)),
+            pltpu.SemaphoreType.DMA((parts + 3,)),
             pltpu.SemaphoreType.DMA((parts, 2)),
+            pltpu.SemaphoreType.DMA((copies,)),
         ],
         cost_estimate=pl.CostEstimate(
             flops=2 * rows * width * 4 * DH, bytes_accessed=4 << 20, transcendentals=rows * 4 * DH
         ),
         compiler_params=pltpu.CompilerParams(vmem_limit_bytes=20 << 20),
         name="project",
-    )(*[pltpu.with_memory_space_constraint(value, pltpu.HBM) for value in (events, in_gain[None], w)])
+    )(
+        place,
+        *[pltpu.with_memory_space_constraint(value, pltpu.HBM) for value in (events, in_gain[None], w, w_out)],
+    )
 
 
 def attend_kernel(users, pieces, count, first, last, place_ref, lengths_ref, q_own, q_sib, *refs):
     blocks, refs = refs[:count], refs[count:]
     if first:
-        out_hbm, total_out, starts_ref, spread_ref, q_ref, total_ref, sems = refs
+        total_out, starts_ref, q_ref, total_ref = refs
         outs = [total_out]
-        copies, _, half = spread_ref.shape
-        columns = pl.ds(pl.multiple_of(place_ref[0] % 2 * half, half), half)
-        spreads = [
-            pltpu.make_async_copy(out_hbm.at[0, :, columns], spread_ref.at[copy], sems.at[copy])
-            for copy in range(copies)
-        ]
-        for spread in spreads:
-            spread.start()
     else:
         starts_ref, carried = refs[:2]
         outs, (q_ref, total_ref) = refs[2:-2], refs[-2:]
@@ -205,9 +214,6 @@
         return nothing
 
     lax.fori_loop(0, 2 * ROWS // TQ, one_part, 0)
-    if first:
-        for spread in spreads:
-            spread.wait()
     if last:
         outs[0][...] = total_ref[:ROWS, :]
         outs[1][...] = total_ref[ROWS:, :].astype(BF16)
@@ -215,7 +221,7 @@
         outs[0][...] = total_ref[...]
 
 
-def attend(place, lengths, q_own, q_sib, blocks, carried=None, weight=1, last=False, w_out=None, copies=1):
+def attend(place, lengths, q_own, q_sib, blocks, carried=None, weight=1, last=False):
     count = len(blocks)
     first = carried is None
     pieces = [
@@ -227,7 +233,6 @@
         outs = [
             pltpu.VMEM((2 * ROWS, DH), F32),
             pltpu.VMEM((2 * ROWS, DH), jnp.int32),
-            pltpu.HBM((copies, DH, w_out.shape[2] // 2), BF16),
         ]
     elif last:
         outs = [pltpu.VMEM((ROWS, DH), F32), pltpu.VMEM((ROWS, DH), BF16)]
@@ -236,14 +241,10 @@
     arrays = kept(q_own, q_sib, *[block[0] for block in blocks], *(() if first else carried))
     specs = [SMEM, SMEM] + [VMEM] * len(arrays)
     scratch = [pltpu.VMEM((2 * ROWS, DH), BF16), pltpu.VMEM((2 * ROWS, DH), F32)]
-    if first:
-        arrays.append(pltpu.with_memory_space_constraint(w_out, pltpu.HBM))
-        specs.append(pl.BlockSpec(memory_space=pltpu.HBM))
-        scratch.append(pltpu.SemaphoreType.DMA((copies,)))
     return pl.pallas_call(
         functools.partial(attend_kernel, lengths.shape[0], pieces, count, first, last),
         in_specs=specs,
-        out_specs=[VMEM, VMEM, pl.BlockSpec(memory_space=pltpu.HBM)] if first else [VMEM] * len(outs),
+        out_specs=[VMEM] * len(outs),
         out_shape=outs,
         scratch_shapes=scratch,
         compiler_params=pltpu.CompilerParams(vmem_limit_bytes=20 << 20),
@@ -323,14 +324,11 @@
     def swapped(value):
         return lax.ppermute(value, "wide", [(i, i ^ 1) for i in range(count)])
 
-    kv, q, u = project(events, in_gain, w_uvqk[:, 0, :])
+    kv, q, u, spread = project(place, events, in_gain, w_uvqk[:, 0, :], w_out, heads)
     q_sib = swapped(q)
     back1 = moved(kv, 2)
     back4 = moved(kv, 8)
-    acc, starts, spread = attend(
-        place, lengths, q, q_sib, [(kv, 0)], weight=0, w_out=w_out, copies=heads
-    )
-    spread, acc = lax.optimization_barrier((spread, acc))
+    acc, starts = attend(place, lengths, q, q_sib, [(kv, 0)], weight=0)
     w_half = lax.all_to_all(spread, "narrow", 0, 0)
     back1, acc = lax.optimization_barrier((back1, acc))
     back2 = moved(back1, 2)

time: 116 us -> 93.7 us (0.81)
  Pallas kernels: 45.2 us -> 16.6 us
  starting transfers between devices: 19.9 us -> 25.3 us
    pallas_call x4, Pallas kernels: 38 us -> 8.8 us  [attend(): pl.pallas_call(functools.partial(attend_kernel, lengths.shape[0], pieces,...]
    ppermute x3, starting transfers between devices: 3.53 us -> 7.14 us  [swapped(): return lax.ppermute(value, 'wide', [(i, i ^ 1) for i in range(count)])]
    ppermute x4, waiting for transfers between devices: 6.33 us -> 9.8 us  [moved(): return lax.ppermute(value, 'wide', pairs)]
    all_to_all x1, waiting for transfers between devices: 10.3 us -> 7.08 us  [on_device(): w_half = lax.all_to_all(spread, 'narrow', 0, 0)]
    all_to_all x1, starting transfers between devices: 8.18 us -> 10 us  [on_device(): w_half = lax.all_to_all(spread, 'narrow', 0, 0)]
  transfers between devices with their start and end apart: 8 -> 8, of which waited for: 5 -> 5; matrix products, arithmetic and copies ran while one was open for 0% -> 0% of each run, Pallas kernels for 33% -> 10%
where the time goes in v1:
time: 93.7 us; the launch traced here: 93.3 us
  blocking collectives  29.5 us (31%)
  starting transfers between devices  25.3 us (27%)
  waiting for transfers between devices  18.3 us (20%)
  Pallas kernels  16.6 us (18%)
  local copies, waits for them, and re-layouts  3.4 us (4%)
    all_to_all x1, blocking collectives, on_device(): lax.all_to_all(gated.reshape(heads, rows // heads, DH), 'narrow', 0, 0)  14.8 us
    all_to_all x1, blocking collectives, on_device(): return lax.all_to_all(out, 'narrow', 0, 0).reshape(rows, DH)  14.7 us
    all_to_all x1, starting transfers between devices, on_device(): w_half = lax.all_to_all(spread, 'narrow', 0, 0)  10 us
    ppermute x4, waiting for transfers between devices, moved(): return lax.ppermute(value, 'wide', pairs)  9.8 us
    pallas_call x4, Pallas kernels, attend(): pl.pallas_call(functools.partial(attend_kernel, lengths.shape[0], pieces,...  8.8 us
    ppermute x4, starting transfers between devices, moved(): return lax.ppermute(value, 'wide', pairs)  8.2 us
    ppermute x3, starting transfers between devices, swapped(): return lax.ppermute(value, 'wide', [(i, i ^ 1) for i in range(count)])  7.14 us
    all_to_all x1, waiting for transfers between devices, on_device(): w_half = lax.all_to_all(spread, 'narrow', 0, 0)  7.08 us
  transfers between devices with their start and end apart: 8, of which 5 were waited for; matrix products, arithmetic and copies ran while one was open for 0% of the time, Pallas kernels for 10%

profile of v1, /device:TPU:1, one launch (start us, length us, event | category | flops | bytes accessed | tf_op | source)
XLA Modules:
  0.0 93.3 jit_solution(3232687667236454288)
XLA Ops:
  0.1 5.5 %project.1 = (bf16[1024,256]{1,0:T(8,128)(2,1)}, bf16[1024,128]{1,0:T(8,128)(2,1)S(1)}, bf16[1024,128]{1,0:T(8,128)(2,1)}, bf16[8,128,512]{2,1,0:T(8,128)(2,1)}) custom-call(s32[2]{0:T(128)S(1)} %pad_add_fusion.place_ref, bf16[1024,1024]{1,0:T(8,128)(2,1)} %events_hbm.3, f32[1,1024]{1,0:T(1,128)} %bitcast.9, bf16[1024,512]{1,0:T(8,128)(2,1)} %bitcast.8, ...), custom_call_target="tpu_custom_call" | custom-call | flops 1073741824 | bytes 4194304 | tf_op jit(solution)/shard_map/project/pallas_call | solution.py:91
  5.6 2.2 %collective-permute-start.3 = (bf16[1024,256]{1,0:T(8,128)(2,1)}, bf16[1024,256]{1,0:T(8,128)(2,1)}, u32[]{:S(2)}, u32[]{:S(2)}) collective-permute-start(bf16[1024,256]{1,0:T(8,128)(2,1)} %get-tuple-element.19.refs_0_), channel_id=1, source_target_pairs={{0,16},{8,24},{16,32},{24,40},{32,48},{40,56},{48,64},{56,72},{64,... | collective-permute-start | bytes 1572872 | tf_op jit(solution)/shard_map/ppermute | solution.py:322
  7.8 1.2 %collective-permute-start = (bf16[1024,128]{1,0:T(8,128)(2,1)S(1)}, bf16[1024,128]{1,0:T(8,128)(2,1)S(1)}, u32[]{:S(2)}, u32[]{:S(2)}) collective-permute-start(bf16[1024,128]{1,0:T(8,128)(2,1)S(1)} %get-tuple-element.18.q_own), channel_id=1, source_target_pairs={{0,8},{8,0},{16,24},{24,16},{32,40},{40,32},{48,56},{56,48},{64,72... | collective-permute-start | bytes 786440 | tf_op jit(solution)/shard_map/ppermute | solution.py:325
  9.0 1.0 %collective-permute-start.1 = (bf16[1024,256]{1,0:T(8,128)(2,1)}, bf16[1024,256]{1,0:T(8,128)(2,1)}, u32[]{:S(2)}, u32[]{:S(2)}) collective-permute-start(bf16[1024,256]{1,0:T(8,128)(2,1)} %get-tuple-element.19.refs_0_), channel_id=1, source_target_pairs={{0,64},{8,72},{16,80},{24,88},{32,96},{40,104},{48,112},{56,120},{... | collective-permute-start | bytes 1572872 | tf_op jit(solution)/shard_map/ppermute | solution.py:322
  10.2 1.0 %copy-done.2 = bf16[1024,256]{1,0:T(8,128)(2,1)S(1)} copy-done((bf16[1024,256]{1,0:T(8,128)(2,1)S(1)}, bf16[1024,256]{1,0:T(8,128)(2,1)}, u32[]{:S(2)}) %copy-start.2) | copy-done | bytes 524312
  11.2 4.3 %attend.4 = (f32[2048,128]{1,0:T(8,128)S(1)}, s32[2048,128]{1,0:T(8,128)S(1)}) custom-call(s32[2]{0:T(128)S(1)} %pad_add_fusion.place_ref, s32[24]{0:T(128)S(1)} %copy-done.4, bf16[1024,128]{1,0:T(8,128)(2,1)S(1)} %get-tuple-element.18.q_own, bf16[1024,128]{1,0:T(8,128)(2,1)S(1)} %collective-permute-done.q_sib, bf16[1024,256]{1,0:T(8,128)(2,1)S(1)} %copy-done.2), custom_call_target="tpu_custom_call" | custom-call | bytes 4194304 | tf_op jit(solution)/shard_map/attend/pallas_call | solution.py:244
  15.6 0.7 copy-done
  16.3 5.2 %collective-permute-done.3.refs_0_ = bf16[1024,256]{1,0:T(8,128)(2,1)} collective-permute-done((bf16[1024,256]{1,0:T(8,128)(2,1)}, bf16[1024,256]{1,0:T(8,128)(2,1)}, u32[]{:S(2)}, u32[]{:S(2)}) %collective-permute-start.3) | collective-permute-done | bytes 524320 | tf_op jit(solution)/shard_map/ppermute | solution.py:322
  21.4 10.0 %all-to-all-start = ((bf16[8,128,512]{2,1,0:T(8,128)(2,1)}), bf16[8,128,512]{2,1,0:T(8,128)(2,1)S(1)}, u32[]{:S(2)}, u32[]{:S(2)}) async-start(bf16[8,128,512]{2,1,0:T(8,128)(2,1)} %get-tuple-element.17), calls=%async_computation | async-start | bytes 2097152 | tf_op jit(solution)/shard_map/all_to_all | solution.py:332
  31.5 5.0 %collective-permute-start.2 = (bf16[1024,256]{1,0:T(8,128)(2,1)}, bf16[1024,256]{1,0:T(8,128)(2,1)S(1)}, u32[]{:S(2)}, u32[]{:S(2)}) collective-permute-start(bf16[1024,256]{1,0:T(8,128)(2,1)} %collective-permute-done.1.refs_1_), channel_id=1, source_target_pairs={{0,240},{8,248},{16,0},{24,8},{32,16},{40,24},{48,32},{56,40},{64,... | collective-permute-start | bytes 1572872 | tf_op jit(solution)/shard_map/ppermute | solution.py:322
  36.5 0.9 %copy-done.1 = bf16[1024,128]{1,0:T(8,128)(2,1)S(1)} copy-done((bf16[1024,128]{1,0:T(8,128)(2,1)S(1)}, bf16[1024,128]{1,0:T(8,128)(2,1)}, u32[]{:S(2)}) %copy-start.1) | copy-done | bytes 262168
  37.4 1.8 %attend.5.refs_2_ = f32[2048,128]{1,0:T(8,128)S(1)} custom-call(s32[2]{0:T(128)S(1)} %pad_add_fusion.place_ref, s32[24]{0:T(128)S(1)} %copy-done.4, bf16[1024,128]{1,0:T(8,128)(2,1)S(1)} %get-tuple-element.18.q_own, bf16[1024,128]{1,0:T(8,128)(2,1)S(1)} %copy-done.1, bf16[1024,256]{1,0:T(8,128)(2,1)} %collective-permute-done.3.refs_0_, ...), custom_call_target="tpu_custom_call" | custom-call | bytes 4194304 | tf_op jit(solution)/shard_map/attend/pallas_call | solution.py:244
  39.3 4.6 %collective-permute-done.4.refs_0_ = bf16[1024,256]{1,0:T(8,128)(2,1)} collective-permute-done((bf16[1024,256]{1,0:T(8,128)(2,1)}, bf16[1024,256]{1,0:T(8,128)(2,1)}, u32[]{:S(2)}, u32[]{:S(2)}) %collective-permute-start.4) | collective-permute-done | bytes 524320 | tf_op jit(solution)/shard_map/ppermute | solution.py:322
  43.9 1.6 %attend.6.refs_2_ = f32[2048,128]{1,0:T(8,128)S(1)} custom-call(s32[2]{0:T(128)S(1)} %pad_add_fusion.place_ref, s32[24]{0:T(128)S(1)} %copy-done.4, bf16[1024,128]{1,0:T(8,128)(2,1)S(1)} %get-tuple-element.18.q_own, bf16[1024,128]{1,0:T(8,128)(2,1)S(1)} %copy-done.1, bf16[1024,256]{1,0:T(8,128)(2,1)} %collective-permute-done.4.refs_0_, ...), custom_call_target="tpu_custom_call" | custom-call | flops 53687091200 | bytes 4194304 | tf_op jit(solution)/shard_map/attend/pallas_call | solution.py:244
  45.5 1.1 %attend.7 = (f32[1024,128]{1,0:T(8,128)S(1)}, bf16[1024,128]{1,0:T(8,128)(2,1)S(1)}) custom-call(s32[2]{0:T(128)S(1)} %pad_add_fusion.place_ref, s32[24]{0:T(128)S(1)} %copy-done.4, bf16[1024,128]{1,0:T(8,128)(2,1)S(1)} %get-tuple-element.18.q_own, bf16[1024,128]{1,0:T(8,128)(2,1)S(1)} %copy-done.1, bf16[1024,256]{1,0:T(8,128)(2,1)S(1)} %collective-permute-done.2.refs_0_, ...), custom_call_target="tpu_custom_call" | custom-call | flops 53687091200 | bytes 4194304 | tf_op jit(solution)/shard_map/attend/pallas_call | solution.py:244
  46.6 3.5 %collective-permute-start.5 = (bf16[1024,128]{1,0:T(8,128)(2,1)S(1)}, bf16[1024,128]{1,0:T(8,128)(2,1)S(1)}, u32[]{:S(2)}, u32[]{:S(2)}) collective-permute-start(bf16[1024,128]{1,0:T(8,128)(2,1)S(1)} %get-tuple-element.25), channel_id=1, source_target_pairs={{0,8},{8,0},{16,24},{24,16},{32,40},{40,32},{48,56},{56,48},{64,72... | collective-permute-start | bytes 786440 | tf_op jit(solution)/shard_map/ppermute | solution.py:325
  50.1 1.2 %collective-permute-done.5.sib_ref = bf16[1024,128]{1,0:T(8,128)(2,1)S(1)} collective-permute-done((bf16[1024,128]{1,0:T(8,128)(2,1)S(1)}, bf16[1024,128]{1,0:T(8,128)(2,1)S(1)}, u32[]{:S(2)}, u32[]{:S(2)}) %collective-permute-start.5) | collective-permute-done | bytes 262176 | tf_op jit(solution)/shard_map/ppermute | solution.py:325
  51.3 0.4 gate.1
  51.6 7.1 %all-to-all-done.mine_ref = bf16[8,128,512]{2,1,0:T(8,128)(2,1)S(1)} async-done(((bf16[8,128,512]{2,1,0:T(8,128)(2,1)}), bf16[8,128,512]{2,1,0:T(8,128)(2,1)S(1)}, u32[]{:S(2)}, u32[]{:S(2)}) %all-to-all-start) | async-done | bytes 1048608 | tf_op jit(solution)/shard_map/all_to_all | solution.py:332
  58.7 2.4 %collective-permute-start.6 = (bf16[8,128,512]{2,1,0:T(8,128)(2,1)S(1)}, bf16[8,128,512]{2,1,0:T(8,128)(2,1)S(1)}, u32[]{:S(2)}, u32[]{:S(2)}) collective-permute-start(bf16[8,128,512]{2,1,0:T(8,128)(2,1)S(1)} %all-to-all-done.mine_ref), channel_id=1, source_target_pairs={{0,8},{8,0},{16,24},{24,16},{32,40},{40,32},{48,56},{56,48},{64,72... | collective-permute-start | bytes 3145736 | tf_op jit(solution)/shard_map/ppermute | solution.py:325
  61.1 14.8 %all_to_all.15.gated_ref = bf16[8,128,128]{2,1,0:T(8,128)(2,1)S(1)} all-to-all(bf16[8,128,128]{2,1,0:T(8,128)(2,1)S(1)} %bitcast.6), channel_id=1, replica_groups=mesh['wide'=32,'narrow'=8] {'narrow'}, dimensions={0} | all-to-all | bytes 524288 | tf_op jit(solution)/shard_map/all_to_all | solution.py:342
  75.9 2.0 %combine.1 = bf16[8,128,128]{2,1,0:T(8,128)(2,1)S(1)} custom-call(s32[2]{0:T(128)S(1)} %pad_add_fusion.place_ref, bf16[8,128,128]{2,1,0:T(8,128)(2,1)S(1)} %all_to_all.15.gated_ref, bf16[8,128,512]{2,1,0:T(8,128)(2,1)S(1)} %all-to-all-done.mine_ref, bf16[8,128,512]{2,1,0:T(8,128)(2,1)S(1)} %collective-permute-done.6.other_ref, bf16[1024,1024]{1,0:T(8,128)(2,1)} %events_hbm.3), custom_call_target="tpu_custom_call" | custom-call | tf_op jit(solution)/shard_map/combine/pallas_call | solution.py:303
  77.9 14.7 %all_to_all.16 = bf16[8,128,128]{2,1,0:T(8,128)(2,1)S(1)} all-to-all(bf16[8,128,128]{2,1,0:T(8,128)(2,1)S(1)} %combine.1), channel_id=1, replica_groups=mesh['wide'=32,'narrow'=8] {'narrow'}, dimensions={0} | all-to-all | bytes 524288 | tf_op jit(solution)/shard_map/all_to_all | solution.py:344
  92.6 0.7 copy.8
  (15 shorter events, 0.3 us)
Async XLA Ops:
  0.0 10.2 %copy-start.4 = (s32[24]{0:T(128)S(1)}, s32[24]{0:T(128)}, u32[]{:S(2)}) copy-start(s32[24]{0:T(128)} %lengths_ref.7) | copy-start | bytes 292
  5.6 15.9 %collective-permute-start.3 = (bf16[1024,256]{1,0:T(8,128)(2,1)}, bf16[1024,256]{1,0:T(8,128)(2,1)}, u32[]{:S(2)}, u32[]{:S(2)}) collective-permute-start(bf16[1024,256]{1,0:T(8,128)(2,1)} %get-tuple-element.19.refs_0_), channel_id=1, source_target_pairs={{0,16},{8,24},{16,32},{24,40},{32,48},{40,56},{48,64},{56,72},{64,... | collective-permute-start | bytes 1572872 | tf_op jit(solution)/shard_map/ppermute | solution.py:322
  7.8 2.4 %collective-permute-start = (bf16[1024,128]{1,0:T(8,128)(2,1)S(1)}, bf16[1024,128]{1,0:T(8,128)(2,1)S(1)}, u32[]{:S(2)}, u32[]{:S(2)}) collective-permute-start(bf16[1024,128]{1,0:T(8,128)(2,1)S(1)} %get-tuple-element.18.q_own), channel_id=1, source_target_pairs={{0,8},{8,0},{16,24},{24,16},{32,40},{40,32},{48,56},{56,48},{64,72... | collective-permute-start | bytes 786440 | tf_op jit(solution)/shard_map/ppermute | solution.py:325
  9.0 22.4 %collective-permute-start.1 = (bf16[1024,256]{1,0:T(8,128)(2,1)}, bf16[1024,256]{1,0:T(8,128)(2,1)}, u32[]{:S(2)}, u32[]{:S(2)}) collective-permute-start(bf16[1024,256]{1,0:T(8,128)(2,1)} %get-tuple-element.19.refs_0_), channel_id=1, source_target_pairs={{0,64},{8,72},{16,80},{24,88},{32,96},{40,104},{48,112},{56,120},{... | collective-permute-start | bytes 1572872 | tf_op jit(solution)/shard_map/ppermute | solution.py:322
  10.2 1.0 %copy-start.2 = (bf16[1024,256]{1,0:T(8,128)(2,1)S(1)}, bf16[1024,256]{1,0:T(8,128)(2,1)}, u32[]{:S(2)}) copy-start(bf16[1024,256]{1,0:T(8,128)(2,1)} %get-tuple-element.19.refs_0_) | copy-start | bytes 1572868
  15.6 0.7 copy-start
  21.4 22.5 %collective-permute-start.4 = (bf16[1024,256]{1,0:T(8,128)(2,1)}, bf16[1024,256]{1,0:T(8,128)(2,1)}, u32[]{:S(2)}, u32[]{:S(2)}) collective-permute-start(bf16[1024,256]{1,0:T(8,128)(2,1)} %collective-permute-done.3.refs_0_), channel_id=1, source_target_pairs={{0,16},{8,24},{16,32},{24,40},{32,48},{40,56},{48,64},{56,72},{64,... | collective-permute-start | bytes 1572872 | tf_op jit(solution)/shard_map/ppermute | solution.py:322
  21.4 37.3 %all-to-all-start = ((bf16[8,128,512]{2,1,0:T(8,128)(2,1)}), bf16[8,128,512]{2,1,0:T(8,128)(2,1)S(1)}, u32[]{:S(2)}, u32[]{:S(2)}) async-start(bf16[8,128,512]{2,1,0:T(8,128)(2,1)} %get-tuple-element.17), calls=%async_computation | async-start | bytes 2097152 | tf_op jit(solution)/shard_map/all_to_all | solution.py:332
  31.5 14.1 %collective-permute-start.2 = (bf16[1024,256]{1,0:T(8,128)(2,1)}, bf16[1024,256]{1,0:T(8,128)(2,1)S(1)}, u32[]{:S(2)}, u32[]{:S(2)}) collective-permute-start(bf16[1024,256]{1,0:T(8,128)(2,1)} %collective-permute-done.1.refs_1_), channel_id=1, source_target_pairs={{0,240},{8,248},{16,0},{24,8},{32,16},{40,24},{48,32},{56,40},{64,... | collective-permute-start | bytes 1572872 | tf_op jit(solution)/shard_map/ppermute | solution.py:322
  36.5 0.9 %copy-start.1 = (bf16[1024,128]{1,0:T(8,128)(2,1)S(1)}, bf16[1024,128]{1,0:T(8,128)(2,1)}, u32[]{:S(2)}) copy-start(bf16[1024,128]{1,0:T(8,128)(2,1)} %copy-done) | copy-start | bytes 786436
  45.5 5.8 %copy-start.3 = (bf16[1024,128]{1,0:T(8,128)(2,1)S(1)}, bf16[1024,128]{1,0:T(8,128)(2,1)}, u32[]{:S(2)}) copy-start(bf16[1024,128]{1,0:T(8,128)(2,1)} %get-tuple-element.26.u_ref) | copy-start | bytes 786436
  45.5 5.8 %copy-start.5 = (f32[1,128]{1,0:T(1,128)S(1)}, f32[1,128]{1,0:T(1,128)}, u32[]{:S(2)}) copy-start(f32[1,128]{1,0:T(1,128)} %gain_ref.1) | copy-start | bytes 1540
  46.6 4.7 %collective-permute-start.5 = (bf16[1024,128]{1,0:T(8,128)(2,1)S(1)}, bf16[1024,128]{1,0:T(8,128)(2,1)S(1)}, u32[]{:S(2)}, u32[]{:S(2)}) collective-permute-start(bf16[1024,128]{1,0:T(8,128)(2,1)S(1)} %get-tuple-element.25), channel_id=1, source_target_pairs={{0,8},{8,0},{16,24},{24,16},{32,40},{40,32},{48,56},{56,48},{64,72... | collective-permute-start | bytes 786440 | tf_op jit(solution)/shard_map/ppermute | solution.py:325
  58.7 17.2 %collective-permute-start.6 = (bf16[8,128,512]{2,1,0:T(8,128)(2,1)S(1)}, bf16[8,128,512]{2,1,0:T(8,128)(2,1)S(1)}, u32[]{:S(2)}, u32[]{:S(2)}) collective-permute-start(bf16[8,128,512]{2,1,0:T(8,128)(2,1)S(1)} %all-to-all-done.mine_ref), channel_id=1, source_target_pairs={{0,8},{8,0},{16,24},{24,16},{32,40},{40,32},{48,56},{56,48},{64,72... | collective-permute-start | bytes 3145736 | tf_op jit(solution)/shard_map/ppermute | solution.py:325
